TPU v7x, 128 devices: a whole 4x4x4 slice. The times are simulated.
128 devices in a mesh: dp: 32 (over y, z, core), tensor: 4 (over x).
Axes of the slice: x: 4, y: 4, z: 4, core: 2. Of those that a mesh axis runs over, the one named last changes fastest.
Arguments:
- queries: bfloat16 [4096, 4096], P('dp', 'tensor'), may hold values from -120 to 120
- token_keys: bfloat16 [4096, 512], P('dp', 'tensor'), may hold values from -4 to 4
- token_values: bfloat16 [4096, 512], P('dp', 'tensor'), may hold values from -4 to 4
- cached_key_rows: bfloat16 [4096, 256, 512], P('dp', None, 'tensor'), may hold values from -4 to 4
- cached_value_rows: bfloat16 [4096, 256, 512], P('dp', None, 'tensor'), may hold values from -4 to 4
- cache_length: int32 [4096], P('dp'), may hold values from 2 to 256, as said below
- output_projection: bfloat16 [4096, 8192], P(None, 'tensor'), may hold values from -0.75 to 0.75
- request_adapter: int32 [4096], P('dp'), may hold values from 0 to 31, as said below
- adapter_table_row: int32 [32], replicated, may hold values from 0 to 31, each once
- adapter_down_weight: bfloat16 [32, 64, 4096], P('dp', None, 'tensor'), may hold values from -0.75 to 0.75
- adapter_up_weight: bfloat16 [32, 64, 8192], P('dp', None, 'tensor'), may hold values from -0.75 to 0.75
Outputs:
- mixed: bfloat16 [4096, 8192], P('dp', 'tensor')
Inputs may be any that keep to these rules, and one draw needn't show every extreme that they name: `cache_length`: at least one request has exactly 256 used positions. `request_adapter`: among the 128 requests of one index of dp no adapter id occurs more than 8 times; in every draw one adapter id occurs exactly 8 times on every index of dp. `adapter_table_row`: each row 0 to 31 is named once.
All inputs are finite; a program needn't handle non-finite values.
Results may differ from a plain program's by a relative error of at most 0.01.
Values may be sent and summed in bfloat16 or wider, within the bound.
No kernel may reach another device: no remote copies, remote signals or barrier semaphores. Data moves between devices by JAX's collectives and lax.ppermute only.
A program may use at most 128 MiB of HBM per device.

v0:
```python
import math
import jax
import jax.numpy as jnp
from jax import lax
from jax.sharding import PartitionSpec as P

HEADS = 32
KV_HEADS = 4
HEAD_DIM = 128


def attend(queries, token_keys, token_values, cached_key_rows, cached_value_rows, cache_length):
    requests = queries.shape[0]
    kv_local = token_keys.shape[1] // HEAD_DIM
    per_group = HEADS // KV_HEADS
    positions = cached_key_rows.shape[1]
    score_scale = 1.0 / math.sqrt(HEAD_DIM)
    query_heads = queries.reshape(requests, kv_local, per_group, HEAD_DIM)
    key_blocks = cached_key_rows.reshape(requests, positions, kv_local, HEAD_DIM)
    value_blocks = cached_value_rows.reshape(requests, positions, kv_local, HEAD_DIM)
    fresh_keys = token_keys.reshape(requests, kv_local, HEAD_DIM)
    fresh_values = token_values.reshape(requests, kv_local, HEAD_DIM)
    cached_score = (
        jnp.einsum("rkgd,rpkd->rkgp", query_heads, key_blocks, preferred_element_type=jnp.float32)
        * score_scale
    )
    fresh_score = (
        jnp.einsum("rkgd,rkd->rkg", query_heads, fresh_keys, preferred_element_type=jnp.float32)
        * score_scale
    )
    in_cache = (jnp.arange(positions, dtype=jnp.int32)[None, :] < cache_length[:, None])[
        :, None, None, :
    ]
    row_max = jnp.maximum(
        jnp.max(jnp.where(in_cache, cached_score, -jnp.inf), axis=-1), fresh_score
    )
    cached_weight = jnp.where(in_cache, jnp.exp(cached_score - row_max[..., None]), 0.0)
    fresh_weight = jnp.exp(fresh_score - row_max)
    weight_sum = jnp.sum(cached_weight, axis=-1) + fresh_weight
    combined = jnp.einsum(
        "rkgp,rpkd->rkgd",
        cached_weight.astype(jnp.bfloat16),
        value_blocks,
        preferred_element_type=jnp.float32,
    )
    combined = combined + jnp.einsum(
        "rkg,rkd->rkgd",
        fresh_weight.astype(jnp.bfloat16),
        fresh_values,
        preferred_element_type=jnp.float32,
    )
    return (
        (combined / weight_sum[..., None])
        .reshape(requests, kv_local * per_group * HEAD_DIM)
        .astype(jnp.bfloat16)
    )


def on_device(
    queries,
    token_keys,
    token_values,
    cached_key_rows,
    cached_value_rows,
    cache_length,
    output_projection,
    request_adapter,
    adapter_table_row,
    adapter_down_weight,
    adapter_up_weight,
):
    attention_output = attend(
        queries, token_keys, token_values, cached_key_rows, cached_value_rows, cache_length
    )
    requests = attention_output.shape[0]
    feature_cols = attention_output.shape[1]
    projected = jnp.dot(
        lax.all_gather(attention_output, "tensor", axis=1, tiled=True),
        output_projection,
        preferred_element_type=jnp.float32,
    )
    every_adapter = adapter_table_row.shape[0]
    table_capacity = 2 * requests // every_adapter
    matches = request_adapter[:, None] == jnp.arange(every_adapter, dtype=jnp.int32)[None, :]
    slot_of = jnp.sum(jnp.where(matches, adapter_table_row[None, :], 0), axis=1)
    request_order = jnp.arange(requests, dtype=jnp.int32)
    earlier = (slot_of[:, None] == slot_of[None, :]) & (
        request_order[:, None] > request_order[None, :]
    )
    position = slot_of * table_capacity + jnp.sum(earlier.astype(jnp.int32), axis=1)
    placing = (
        jnp.arange(every_adapter * table_capacity, dtype=jnp.int32)[:, None] == position[None, :]
    ).astype(jnp.bfloat16)
    buffer_rows = jnp.dot(placing, attention_output, preferred_element_type=jnp.float32).astype(
        jnp.bfloat16
    )
    table_down, table_up = (
        lax.all_gather(adapter_down_weight, "dp", axis=0, tiled=True),
        lax.all_gather(adapter_up_weight, "dp", axis=0, tiled=True),
    )
    grouped = buffer_rows.reshape(every_adapter, table_capacity, feature_cols)
    rank_terms = jnp.einsum("acw,arw->acr", grouped, table_down, preferred_element_type=jnp.float32)
    low_rank_state = lax.psum(rank_terms, "tensor").astype(jnp.bfloat16)
    adapter_deltas = jnp.einsum(
        "acr,ard->acd", low_rank_state, table_up, preferred_element_type=jnp.float32
    ).astype(jnp.bfloat16)
    adapter_deltas = adapter_deltas.reshape(
        every_adapter * table_capacity, adapter_up_weight.shape[2]
    )
    returned = jnp.einsum("sr,sd->rd", placing, adapter_deltas, preferred_element_type=jnp.float32)
    return (projected + returned).astype(jnp.bfloat16)


def solution(mesh):
    in_specs = (
        P("dp", "tensor"),
        P("dp", "tensor"),
        P("dp", "tensor"),
        P("dp", None, "tensor"),
        P("dp", None, "tensor"),
        P("dp"),
        P(None, "tensor"),
        P("dp"),
        P(),
        P("dp", None, "tensor"),
        P("dp", None, "tensor"),
    )
    out_specs = P("dp", "tensor")
    return jax.shard_map(
        on_device, mesh=mesh, in_specs=in_specs, out_specs=out_specs, check_vma=False
    )
```

profile of v0, /device:TPU:1, one launch (start us, length us, event | category | flops | bytes accessed | tf_op | source)
XLA Modules:
  0.0 161.0 jit_solution(15225295024856014704)
XLA Ops:
  6.5 0.0 all-gather.4.cloned.1.call-start
  6.5 0.9 iota_compare_fusion.4
  7.4 1.4 copy.14
  8.9 0.3 fusion.17
  9.1 5.7 %select_reduce_fusion = (f32[128,8]{1,0:T(8,128)S(1)}, f32[128,8,256]{2,1,0:T(8,128)S(1)}) fusion(pred[128,256]{1,0:T(8,128)(4,1)S(1)} %iota_compare_fusion.4, bf16[128,8,128]{2,1,0:T(8,128)(2,1)S(1)} %bitcast.32, bf16[128,256,128]{2,1,0:T(8,128)(2,1)} %param.14), kind=kOutput, calls=%fused_computation.11 | convolution fusion | flops 67894272 | bytes 9736192 | tf_op jit(solution)/shard_map/rkgd,rpkd->rkgp/dot_general | solution.py:24
  14.9 0.4 fusion.5
  15.3 0.0 copy-done.1
  15.4 0.0 copy-done.2
  15.4 1.3 fusion.4
  16.7 0.8 copy.21
  17.4 0.0 all-gather.4.cloned.1.call-update
  17.5 0.0 all-gather.6.cloned.1.call-start
  17.5 0.7 all-gather.6.cloned.1.call-update
  18.2 0.0 all-gather.8.cloned.1.call-start
  18.3 0.7 all-gather.8.cloned.1.call-update
  19.0 0.1 select_reduce_fusion.1
  19.1 0.2 convert_reduce_fusion
  19.2 24.6 %all-gather.4.cloned.1.call-done = bf16[128,4096]{1,0:T(8,128)(2,1)} async-done(((bf16[128,1024]{1,0:T(8,128)(2,1)}), bf16[128,4096]{1,0:T(8,128)(2,1)}) %all-gather.4.cloned.1.call-update) | async-done | bytes 1048592 | tf_op jit(solution)/shard_map/all_gather | solution.py:78
  43.9 8.4 %fusion.22 = f32[128,2048]{1,0:T(8,128)S(1)} fusion(bf16[128,4096]{1,0:T(8,128)(2,1)} %all-gather.4.cloned.1.call-done, bf16[4096,2048]{1,0:T(8,128)(2,1)} %param.17), kind=kOutput, calls=%fused_computation.37 | convolution fusion | flops 2147483648 | bytes 18874368 | tf_op jit(solution)/shard_map/dot_general | solution.py:77
  52.3 41.9 %all-gather.6.cloned.1.call-done = bf16[32,64,1024]{2,1,0:T(8,128)(2,1)} async-done(((bf16[1,64,1024]{2,1,0:T(8,128)(2,1)}), bf16[32,64,1024]{2,1,0:T(8,128)(2,1)}) %all-gather.6.cloned.1.call-update) | async-done | bytes 4194320 | tf_op jit(solution)/shard_map/all_gather | solution.py:98
  94.2 3.5 %fusion.7 = f32[32,8,64]{2,1,0:T(8,128)S(1)} fusion(bf16[32,64,1024]{2,1,0:T(8,128)(2,1)} %all-gather.6.cloned.1.call-done, s32[128]{0:T(128)S(1)} %multiply_add_fusion, bf16[16,8,8,128]{3,2,1,0:T(8,128)(2,1)S(1)} %bitcast.30), kind=kOutput, calls=%fused_computation.14 | convolution fusion | flops 100958208 | bytes 4522496 | tf_op jit(solution)/shard_map/acw,arw->acr/dot_general | solution.py:102
  97.8 14.6 %psum.7 = bf16[32,8,64]{2,1,0:T(8,128)(2,1)S(1)} all-reduce(f32[32,8,64]{2,1,0:T(8,128)S(1)} %fusion.7), channel_id=1, replica_groups=mesh['dp'=32,'tensor'=4] {'tensor'}, use_global_device_ids=true, to_apply=%region_4.5 | all-reduce | flops 16384 | bytes 98304 | tf_op jit(solution)/shard_map/psum | solution.py:103
  112.3 36.5 %all-gather.8.cloned.1.call-done = bf16[32,64,2048]{2,1,0:T(8,128)(2,1)} async-done(((bf16[1,64,2048]{2,1,0:T(8,128)(2,1)}), bf16[32,64,2048]{2,1,0:T(8,128)(2,1)}) %all-gather.8.cloned.1.call-update) | async-done | bytes 8388624 | tf_op jit(solution)/shard_map/all_gather | solution.py:99
  148.8 5.6 %fusion.1 = bf16[128,2048]{1,0:T(8,128)(2,1)} fusion(f32[128,2048]{1,0:T(8,128)S(1)} %fusion.22, bf16[32,64,2048]{2,1,0:T(8,128)(2,1)} %all-gather.8.cloned.1.call-done, bf16[32,8,64]{2,1,0:T(8,128)(2,1)S(1)} %psum.7, s32[128]{0:T(128)S(1)} %multiply_add_fusion), kind=kOutput, calls=%fused_computation.3 | convolution fusion | flops 202407936 | bytes 9994752 | tf_op jit(solution)/shard_map/sr,sd->rd/dot_general | solution.py:110
  (12 shorter events, 0.1 us)
Async XLA Ops:
  6.5 2.3 %copy-start = (bf16[128,128]{1,0:T(8,128)(2,1)S(1)}, bf16[128,128]{1,0:T(8,128)(2,1)}, u32[]{:S(2)}) copy-start(bf16[128,128]{1,0:T(8,128)(2,1)} %param.12) | copy-start | bytes 98308
  6.5 8.8 %copy-start.1 = (bf16[128,128]{1,0:T(8,128)(2,1)S(1)}, bf16[128,128]{1,0:T(8,128)(2,1)}, u32[]{:S(2)}) copy-start(bf16[128,128]{1,0:T(8,128)(2,1)} %param.13) | copy-start | bytes 98308
  6.5 37.3 %all-gather.4.cloned.1.call-start = ((), (), s32[]{:S(2)}) async-start(), calls=%async_computation | async-start | bytes 1310720 | tf_op jit(solution)/shard_map/all_gather | solution.py:78
  6.5 8.8 %copy-start.2 = (bf16[128,256,128]{2,1,0:T(8,128)(2,1)S(1)}, bf16[128,256,128]{2,1,0:T(8,128)(2,1)}, u32[]{:S(2)}) copy-start(bf16[128,256,128]{2,1,0:T(8,128)(2,1)} %param.15) | copy-start | bytes 25165828
  14.9 4.1 %copy-start.3 = (s32[32]{0:T(128)S(1)}, s32[32]{0:T(128)}, u32[]{:S(2)}) copy-start(s32[32]{0:T(128)} %param.19) | copy-start | bytes 388
  14.9 4.1 %copy-start.4 = (s32[128]{0:T(128)S(1)}, s32[128]{0:T(128)}, u32[]{:S(2)}) copy-start(s32[128]{0:T(128)} %param.18) | copy-start | bytes 1540
  17.5 76.8 %all-gather.6.cloned.1.call-start = ((), (), s32[]{:S(2)}) async-start(), calls=%async_computation.1 | async-start | bytes 4325376 | tf_op jit(solution)/shard_map/all_gather | solution.py:98
  18.2 130.6 %all-gather.8.cloned.1.call-start = ((), (), s32[]{:S(2)}) async-start(), calls=%async_computation.2 | async-start | bytes 8650752 | tf_op jit(solution)/shard_map/all_gather | solution.py:99
Sparse Core Ops, SparseCore 0:
  17.6 26.2 all-gather.3
  46.1 48.0 all-gather.5
  96.5 52.2 all-gather.7
where the time goes:
time: 161 us
  waiting for transfers between devices  104 us (65%)
  matrix products  24.9 us (15%)
  blocking collectives  14.6 us (9%)
  between operations  13.2 us (8%)
  local copies, waits for them, and re-layouts  2.18 us (1%)
    all_gather x1, waiting for transfers between devices, on_device(): lax.all_gather(adapter_down_weight, 'dp', axis=0, tiled=True)  41.9 us
    all_gather x1, waiting for transfers between devices, on_device(): lax.all_gather(adapter_up_weight, 'dp', axis=0, tiled=True)  36.5 us
    all_gather x1, waiting for transfers between devices, on_device(): lax.all_gather(attention_output, 'tensor', axis=1, tiled=True)  24.6 us
    psum x1, blocking collectives, on_device(): low_rank_state = lax.psum(rank_terms, 'tensor').astype(jnp.bfloat16)  14.6 us
    dot_general x1, matrix products, on_device(): jnp.dot(lax.all_gather(attention_output, 'tensor', axis=1, tiled=True), o...  8.43 us
    dot_general x1, matrix products, attend(): jnp.einsum('rkgd,rpkd->rkgp', query_heads, key_blocks, preferred_element_...  5.74 us
    dot_general x1, matrix products, on_device(): jnp.einsum('sr,sd->rd', placing, adapter_deltas, preferred_element_type=j...  5.62 us
    dot_general x1, matrix products, on_device(): jnp.einsum('acw,arw->acr', grouped, table_down, preferred_element_type=jn...  3.54 us
  transfers between devices with their start and end apart: 3, of which 3 were waited for; matrix products, arithmetic and copies ran while one was open for 8% of the time, Pallas kernels for 0%

commit v1 on v0

--- a/solution.py
+++ b/solution.py
@@ -75,7 +75,10 @@
     requests = attention_output.shape[0]
     feature_cols = attention_output.shape[1]
     projected = jnp.dot(
-        lax.all_gather(attention_output, "tensor", axis=1, tiled=True),
+        jnp.concatenate(
+            lax.all_to_all(jnp.stack([attention_output] * lax.axis_size("tensor")), "tensor", 0, 0),
+            axis=1,
+        ),
         output_projection,
         preferred_element_type=jnp.float32,
     )

time: 161 us -> 127 us (0.79)
  waiting for transfers between devices: 104 us -> 63.5 us
  starting transfers between devices: 0.08 us -> 4.88 us
    all_gather x1, waiting for transfers between devices: 41.9 us -> 11.8 us  [on_device(): lax.all_gather(adapter_down_weight, 'dp', axis=0, tiled=True)]
    all_gather x1 -> x0, waiting for transfers between devices: 24.6 us -> none  [on_device(): lax.all_gather(attention_output, 'tensor', axis=1, tiled=True)]
    all_to_all x0 -> x1, waiting for transfers between devices: none -> 13.9 us  [on_device(): lax.all_to_all(jnp.stack([attention_output] * lax.axis_size('tensor')), '...]
    all_to_all x0 -> x1, starting transfers between devices: none -> 4.84 us  [on_device(): lax.all_to_all(jnp.stack([attention_output] * lax.axis_size('tensor')), '...]
  transfers between devices with their start and end apart: 3 -> 3, of which waited for: 3 -> 3; matrix products, arithmetic and copies ran while one was open for 8% -> 19% of each run, Pallas kernels for 0% -> 0%
where the time goes in v1:
time: 127 us
  waiting for transfers between devices  63.5 us (50%)
  matrix products  24.9 us (20%)
  blocking collectives  14.6 us (11%)
  between operations  13.5 us (11%)
  starting transfers between devices  4.88 us (4%)
  other arithmetic  2.75 us (2%)
  local copies, waits for them, and re-layouts  2.57 us (2%)
    all_gather x1, waiting for transfers between devices, on_device(): lax.all_gather(adapter_up_weight, 'dp', axis=0, tiled=True)  36.5 us
    psum x1, blocking collectives, on_device(): low_rank_state = lax.psum(rank_terms, 'tensor').astype(jnp.bfloat16)  14.6 us
    all_to_all x1, waiting for transfers between devices, on_device(): lax.all_to_all(jnp.stack([attention_output] * lax.axis_size('tensor')), '...  13.9 us
    all_gather x1, waiting for transfers between devices, on_device(): lax.all_gather(adapter_down_weight, 'dp', axis=0, tiled=True)  11.8 us
    dot_general x1, matrix products, on_device(): jnp.dot(jnp.concatenate(lax.all_to_all(jnp.stack([attention_output] * lax...  8.47 us
    dot_general x1, matrix products, attend(): jnp.einsum('rkgd,rpkd->rkgp', query_heads, key_blocks, preferred_element_...  5.74 us
    dot_general x1, matrix products, on_device(): jnp.einsum('sr,sd->rd', placing, adapter_deltas, preferred_element_type=j...  5.62 us
    all_to_all x1, starting transfers between devices, on_device(): lax.all_to_all(jnp.stack([attention_output] * lax.axis_size('tensor')), '...  4.84 us
  transfers between devices with their start and end apart: 3, of which 3 were waited for; matrix products, arithmetic and copies ran while one was open for 19% of the time, Pallas kernels for 0%

profile of v1, /device:TPU:1, one launch (start us, length us, event | category | flops | bytes accessed | tf_op | source)
XLA Modules:
  0.0 126.8 jit_solution(2980121256509311594)
XLA Ops:
  6.5 0.7 all-gather.3.cloned.1.call-update
  7.3 0.0 all-gather.5.cloned.1.call-start
  7.3 0.7 all-gather.5.cloned.1.call-update
  8.0 0.0 copy-start.1
  8.0 1.1 copy.17
  9.2 1.0 convert.7
  10.2 1.0 iota_compare_fusion.4
  11.2 0.3 fusion.17
  11.5 5.7 %select_reduce_fusion = (f32[128,8]{1,0:T(8,128)S(1)}, f32[128,8,256]{2,1,0:T(8,128)S(1)}) fusion(pred[128,256]{1,0:T(8,128)(4,1)S(1)} %iota_compare_fusion.4, bf16[128,8,128]{2,1,0:T(8,128)(2,1)S(1)} %bitcast.36, bf16[128,256,128]{2,1,0:T(8,128)(2,1)} %param.14), kind=kOutput, calls=%fused_computation.11 | convolution fusion | flops 67894272 | bytes 9736192 | tf_op jit(solution)/shard_map/rkgd,rpkd->rkgp/dot_general | solution.py:24
  17.3 0.4 fusion.5
  17.7 1.3 %fusion.4 = bf16[128,8,128]{2,1,0:T(8,128)(2,1)S(1)} fusion(bf16[128,256,128]{2,1,0:T(8,128)(2,1)S(1)} %copy-done.1, f32[128,8,256]{2,1,0:T(8,128)S(1)} %get-tuple-element.8, f32[128,8]{1,0:T(8,128)S(1)} %multiply_maximum_fusion, pred[128,256]{1,0:T(8,128)(4,1)S(1)} %iota_compare_fusion.4, f32[128,8]{1,0:T(8,128)S(1)} %get-tuple-element.6, ...), kind=kOutput, calls=%fused_computation.9 | convolution fusion | flops 68419584 | bytes 9809920 | tf_op jit(solution)/shard_map/rkgp,rpkd->rkgd/dot_general | solution.py:40
  19.0 0.1 copy.24
  19.1 0.2 copy.14
  19.3 1.2 stack.2
  20.4 4.8 %all-to-all-start = ((bf16[4,128,1024]{1,2,0:T(8,128)(2,1)}), bf16[4,128,1024]{1,2,0:T(8,128)(2,1)S(1)}, u32[]{:S(2)}, u32[]{:S(2)}) async-start(bf16[4,128,1024]{1,2,0:T(8,128)(2,1)} %stack.2), calls=%async_computation | async-start | bytes 2097152 | tf_op jit(solution)/shard_map/all_to_all | solution.py:79
  25.3 0.1 select_reduce_fusion.1
  25.4 0.2 convert_reduce_fusion
  25.6 13.9 %all-to-all-done = bf16[4,128,1024]{1,2,0:T(8,128)(2,1)S(1)} async-done(((bf16[4,128,1024]{1,2,0:T(8,128)(2,1)}), bf16[4,128,1024]{1,2,0:T(8,128)(2,1)S(1)}, u32[]{:S(2)}, u32[]{:S(2)}) %all-to-all-start) | async-done | bytes 1048608 | tf_op jit(solution)/shard_map/all_to_all | solution.py:79
  39.5 8.5 %fusion.22 = f32[128,2048]{1,0:T(8,128)S(1)} fusion(bf16[128,4096]{0,1:T(8,128)(2,1)S(1)} %bitcast.32, bf16[4096,2048]{1,0:T(8,128)(2,1)} %param.17), kind=kOutput, calls=%fused_computation.37 | convolution fusion | flops 2147483648 | bytes 18874368 | tf_op jit(solution)/shard_map/dot_general | solution.py:77
  47.9 11.8 %all-gather.3.cloned.1.call-done = bf16[32,64,1024]{2,1,0:T(8,128)(2,1)} async-done(((bf16[1,64,1024]{2,1,0:T(8,128)(2,1)}), bf16[32,64,1024]{2,1,0:T(8,128)(2,1)}) %all-gather.3.cloned.1.call-update) | async-done | bytes 4194320 | tf_op jit(solution)/shard_map/all_gather | solution.py:101
  59.7 3.5 %fusion.7 = f32[32,8,64]{2,1,0:T(8,128)S(1)} fusion(bf16[32,64,1024]{2,1,0:T(8,128)(2,1)} %all-gather.3.cloned.1.call-done, s32[128]{0:T(128)S(1)} %multiply_add_fusion, bf16[16,8,8,128]{3,2,1,0:T(8,128)(2,1)S(1)} %bitcast.34), kind=kOutput, calls=%fused_computation.14 | convolution fusion | flops 100958208 | bytes 4522496 | tf_op jit(solution)/shard_map/acw,arw->acr/dot_general | solution.py:105
  63.2 14.6 %psum.7 = bf16[32,8,64]{2,1,0:T(8,128)(2,1)S(1)} all-reduce(f32[32,8,64]{2,1,0:T(8,128)S(1)} %fusion.7), channel_id=1, replica_groups=mesh['dp'=32,'tensor'=4] {'tensor'}, use_global_device_ids=true, to_apply=%region_4.5 | all-reduce | flops 16384 | bytes 98304 | tf_op jit(solution)/shard_map/psum | solution.py:106
  77.8 36.5 %all-gather.5.cloned.1.call-done = bf16[32,64,2048]{2,1,0:T(8,128)(2,1)} async-done(((bf16[1,64,2048]{2,1,0:T(8,128)(2,1)}), bf16[32,64,2048]{2,1,0:T(8,128)(2,1)}) %all-gather.5.cloned.1.call-update) | async-done | bytes 8388624 | tf_op jit(solution)/shard_map/all_gather | solution.py:102
  114.3 5.6 %fusion.1 = bf16[128,2048]{1,0:T(8,128)(2,1)} fusion(f32[128,2048]{1,0:T(8,128)S(1)} %fusion.22, bf16[32,64,2048]{2,1,0:T(8,128)(2,1)} %all-gather.5.cloned.1.call-done, bf16[32,8,64]{2,1,0:T(8,128)(2,1)S(1)} %psum.7, s32[128]{0:T(128)S(1)} %multiply_add_fusion), kind=kOutput, calls=%fused_computation.3 | convolution fusion | flops 202407936 | bytes 9994752 | tf_op jit(solution)/shard_map/sr,sd->rd/dot_general | solution.py:113
  (11 shorter events, 0.1 us)
Async XLA Ops:
  6.5 4.7 %copy-start = (bf16[128,128]{1,0:T(8,128)(2,1)S(1)}, bf16[128,128]{1,0:T(8,128)(2,1)}, u32[]{:S(2)}) copy-start(bf16[128,128]{1,0:T(8,128)(2,1)} %param.12) | copy-start | bytes 98308
  6.5 53.2 %all-gather.3.cloned.1.call-start = ((), (), s32[]{:S(2)}) async-start(), calls=%async_computation.1 | async-start | bytes 4325376 | tf_op jit(solution)/shard_map/all_gather | solution.py:101
  7.3 107.0 %all-gather.5.cloned.1.call-start = ((), (), s32[]{:S(2)}) async-start(), calls=%async_computation.2 | async-start | bytes 8650752 | tf_op jit(solution)/shard_map/all_gather | solution.py:102
  8.0 9.7 %copy-start.1 = (bf16[128,256,128]{2,1,0:T(8,128)(2,1)S(1)}, bf16[128,256,128]{2,1,0:T(8,128)(2,1)}, u32[]{:S(2)}) copy-start(bf16[128,256,128]{2,1,0:T(8,128)(2,1)} %param.15) | copy-start | bytes 25165828
  17.2 8.0 %copy-start.2 = (s32[32]{0:T(128)S(1)}, s32[32]{0:T(128)}, u32[]{:S(2)}) copy-start(s32[32]{0:T(128)} %param.19) | copy-start | bytes 388
  17.2 8.1 %copy-start.3 = (s32[128]{0:T(128)S(1)}, s32[128]{0:T(128)}, u32[]{:S(2)}) copy-start(s32[128]{0:T(128)} %param.18) | copy-start | bytes 1540
  20.4 19.0 %all-to-all-start = ((bf16[4,128,1024]{1,2,0:T(8,128)(2,1)}), bf16[4,128,1024]{1,2,0:T(8,128)(2,1)S(1)}, u32[]{:S(2)}, u32[]{:S(2)}) async-start(bf16[4,128,1024]{1,2,0:T(8,128)(2,1)} %stack.2), calls=%async_computation | async-start | bytes 2097152 | tf_op jit(solution)/shard_map/all_to_all | solution.py:79
Sparse Core Ops, SparseCore 0:
  9.6 50.0 all-gather.2
  62.0 52.2 all-gather.4
